TPU v7x, 32 devices: a whole 2x2x4 slice. The times are simulated.
32 devices in a mesh: req: 4 (over z), row: 4 (over x, core), col: 2 (over y).
Axes of the slice: x: 2, y: 2, z: 4, core: 2. Of those that a mesh axis runs over, the one named last changes fastest.
Arguments:
- tokens: bfloat16 [1792, 4096], P('col', ('req', 'row')), may hold values from -6 to 6
- qkv_weight: bfloat16 [1792, 2304], P('col', 'row'), may hold values from -0.125 to 0.125
- out_weight: bfloat16 [1792, 1792], P('row', 'col'), may hold values from -0.125 to 0.125
- head_gain: float32 [1792], P('row'), may hold values from 0.1 to 1.9
- prefix_keys: bfloat16 [12, 256, 8192], P('req', 'row', 'col'), may hold values from -6 to 6
- prefix_values: bfloat16 [12, 1792, 8192], P('req', 'row', 'col'), may hold values from -6 to 6
- suffix_len: int32 [8], P(('req', 'col')), may hold values from 1 to 512, 3072 in all
- prefix_owner: int32 [8], P(('req', 'col')), may hold values from 0 to 11
Outputs:
- layer_out: bfloat16 [1792, 4096], P('col', ('req', 'row'))
Inputs may be any that keep to these rules, and one draw needn't show every extreme that they name: `suffix_len`: the longest suffix has exactly 512 live tokens.
All inputs are finite; a program needn't handle non-finite values. No bound on the sum of `suffix_len` on one device may be relied on, other than what follows from the above.
Results may differ from a plain program's by a relative error of at most 0.015.
Values may be sent and summed in bfloat16 or wider, within the bound.
A program may use at most 128 MiB of HBM per device.

v0:
```python
import jax
import jax.numpy as jnp
from jax import lax
from jax.sharding import PartitionSpec as P

FEAT = 16
SLOTS = 512
HD = 112


epsilon = 1e-05


def feature_map(values_in):
    feature_count = values_in.shape[-1]
    squares = (values_in[..., :, None] * values_in[..., None, :]).reshape(
        values_in.shape[:-1] + (feature_count * feature_count,)
    )
    constant = jnp.ones(values_in.shape[:-1] + (1,), jnp.float32)
    linear = values_in * feature_count ** (-0.25)
    quadratic = squares * (0.5**0.5 / feature_count**0.5)
    return jnp.concatenate([constant, linear, quadratic], axis=-1).astype(jnp.bfloat16)


def feature_columns(values_in):
    feature_count = values_in.shape[-2]
    length = values_in.shape[-1]
    squares = (values_in[..., :, None, :] * values_in[..., None, :, :]).reshape(
        values_in.shape[:-2] + (feature_count * feature_count, length)
    )
    constant = jnp.ones(values_in.shape[:-2] + (1, length), jnp.float32)
    linear = values_in * feature_count ** (-0.25)
    quadratic = squares * (0.5**0.5 / feature_count**0.5)
    return jnp.concatenate([constant, linear, quadratic], axis=-2).astype(jnp.bfloat16)


def shards(
    tokens, qkv_weight, out_weight, head_gain, prefix_keys, prefix_values, suffix_len, prefix_owner
):
    heads_here = head_gain.shape[0] // HD
    partial_proj = lax.dot_general(
        lax.all_gather(tokens, "row", axis=1, tiled=True),
        qkv_weight,
        (((0,), (0,)), ((), ())),
        preferred_element_type=jnp.float32,
    )
    projected = lax.psum_scatter(
        partial_proj.astype(jnp.bfloat16), "col", scatter_dimension=0, tiled=True
    )
    requests = projected.shape[0] // SLOTS
    projected = projected.reshape(requests, SLOTS, heads_here, 2 * FEAT + HD)
    queries = projected[..., :FEAT]
    keys_now = projected[..., FEAT : 2 * FEAT]
    values_now = projected[..., 2 * FEAT :]
    pref_here = prefix_keys.shape[0]
    plen_here = prefix_keys.shape[2]
    feats_cached = feature_columns(
        prefix_keys.reshape(pref_here, heads_here, FEAT, plen_here).astype(jnp.float32)
    )
    values_cached = prefix_values.reshape(pref_here, heads_here, HD, plen_here)
    partial_state = jnp.einsum(
        "phet,phvt->phev", feats_cached, values_cached, preferred_element_type=jnp.float32
    )
    summed_state = lax.psum(partial_state.astype(jnp.bfloat16), "col").astype(jnp.float32)
    states = lax.all_gather(summed_state.astype(jnp.bfloat16), "req", axis=0, tiled=True).astype(
        summed_state.dtype
    )
    prefixes = states.shape[0]
    selector = (prefix_owner[:, None] == jnp.arange(prefixes, dtype=jnp.int32)[None, :]).astype(
        jnp.float32
    )
    chosen = jnp.einsum("rp,phev->rhev", selector, states, precision=lax.Precision.HIGHEST)
    feats_query = feature_map(queries.astype(jnp.float32)).astype(jnp.float32)
    carried = jnp.einsum("rthe,rhev->rthv", feats_query, chosen, precision=lax.Precision.HIGHEST)
    scores = jnp.einsum("rthf,rshf->rhts", queries, keys_now, preferred_element_type=jnp.float32)
    weights = 1.0 + scores * FEAT ** (-0.5) + scores * scores * (0.5 / FEAT)
    positions = jnp.arange(SLOTS, dtype=jnp.int32)
    allowed = (positions[None, None, :] <= positions[None, :, None]) & (
        positions[None, None, :] < suffix_len[:, None, None]
    )
    weights = jnp.where(allowed[:, None], weights, 0.0).astype(jnp.bfloat16)
    within = jnp.einsum("rhts,rshv->rthv", weights, values_now, preferred_element_type=jnp.float32)
    active = (positions[None, :] < suffix_len[:, None])[:, :, None, None]
    attended = jnp.where(active, carried + within, 0.0)
    inverse_rms = lax.rsqrt(jnp.mean(attended * attended, axis=-1, keepdims=True) + epsilon)
    gains = head_gain.reshape(heads_here, HD)
    normed = (
        (attended * inverse_rms * gains)
        .astype(jnp.bfloat16)
        .reshape(requests * SLOTS, heads_here * HD)
    )
    out_terms = lax.dot_general(
        out_weight,
        lax.all_gather(normed, "col", axis=0, tiled=True),
        (((0,), (1,)), ((), ())),
        preferred_element_type=jnp.float32,
    )
    mixed_sums = lax.psum_scatter(
        out_terms.astype(jnp.bfloat16), "row", scatter_dimension=1, tiled=True
    ).astype(jnp.float32)
    return (tokens.astype(jnp.float32) + mixed_sums).astype(jnp.bfloat16)


def solution(mesh):
    in_specs = (
        P("col", ("req", "row")),
        P("col", "row"),
        P("row", "col"),
        P("row"),
        P("req", "row", "col"),
        P("req", "row", "col"),
        P(("req", "col")),
        P(("req", "col")),
    )
    out_specs = P("col", ("req", "row"))
    return jax.shard_map(shards, mesh=mesh, in_specs=in_specs, out_specs=out_specs, check_vma=False)
```

profile of v0, /device:TPU:0, one launch (start us, length us, event | category | flops | bytes accessed | tf_op | source)
XLA Modules:
  0.0 226.6 jit_solution(8718943792197056923)
XLA Ops:
  7.4 0.7 all-gather.5.cloned.1.call-update
  8.1 0.0 all-reduce.2.cloned.1.call-start
  8.1 1.7 convert.24
  9.9 11.0 %multiply_convert_fusion = bf16[3,4,16,16,4096]{4,3,2,1,0:T(8,128)(2,1)} fusion(f32[3,4,16,4096]{3,2,1,0:T(8,128)S(1)} %convert.24), kind=kLoop, calls=%fused_computation | loop fusion | flops 37748736 | bytes 28311552 | tf_op jit(solution)/shard_map/convert.9
  20.9 0.4 multiply_convert_fusion.1
  21.3 15.3 %fusion = bf16[3,4,273,112]{3,2,1,0:T(8,128)(2,1)S(1)} fusion(bf16[3,4,112,4096]{3,2,1,0:T(8,128)(2,1)} %bitcast.61, bf16[3,4,256,4096]{3,2,1,0:T(8,128)(2,1)} %bitcast.53, bf16[3,4,16,4096]{3,2,1,0:T(8,128)(2,1)S(1)} %multiply_convert_fusion.1, bf16[273]{0:T(512)(128)(2,1)S(1)} %pad.3.clone), kind=kOutput, calls=%fused_computation.1 | convolution fusion | flops 3086254080 | bytes 38483104 | tf_op jit(solution)/shard_map/phet,phvt->phev/dot_general | solution.py:61
  36.7 1.2 copy.24
  37.9 0.0 all-reduce.2.cloned.1.call-update
  37.9 0.0 reduce-scatter.3.cloned.1.call-start
  38.0 0.0 all-gather.5.cloned.1.call-done
  38.0 3.9 %convolution_convert_fusion = bf16[1024,576]{0,1:T(8,128)(2,1)} fusion(bf16[896,576]{0,1:T(8,128)(2,1)S(1)} %copy-done, bf16[896,1024]{1,0:T(8,128)(2,1)} %all-gather.5.cloned.1.call-done), kind=kOutput, calls=%fused_computation.14 | convolution fusion | flops 1057554432 | bytes 4046848 | tf_op jit(solution)/shard_map/dot_general | solution.py:41
  41.9 0.0 reduce-scatter.3.cloned.1.call-update
  41.9 0.0 all-gather.3.cloned.1.call-start
  42.0 34.0 %all-reduce.2.cloned.1.call-done = bf16[3,4,273,112]{3,1,2,0:T(4,128)(2,1)} async-done(((bf16[3,4,273,112]{3,1,2,0:T(4,128)(2,1)}), bf16[3,4,273,112]{3,1,2,0:T(4,128)(2,1)}) %all-reduce.2.cloned.1.call-update) | async-done | bytes 733840 | tf_op jit(solution)/shard_map/psum | solution.py:64
  76.0 0.0 reduce-scatter.5.cloned.1.call-start
  77.4 0.1 mul.133
  77.5 0.1 fusion.16
  77.5 22.6 %reduce-scatter.3.cloned.1.call-done = bf16[512,576]{0,1:T(8,128)(2,1)} async-done(((bf16[1024,576]{0,1:T(8,128)(2,1)}), bf16[512,576]{0,1:T(8,128)(2,1)}) %reduce-scatter.3.cloned.1.call-update) | async-done | bytes 589840 | tf_op jit(solution)/shard_map/reduce_scatter | solution.py:47
  100.1 0.9 fusion.21
  101.0 0.9 convert_bitcast_fusion.1
  101.9 0.3 multiply_convert_fusion.2
  102.1 2.7 %fusion.8 = f32[4,112,512]{2,1,0:T(8,128)S(1)} fusion(pred[512,512]{1,0:T(8,128)(4,1)S(1)} %fusion.16, bf16[1,512,4,144]{1,3,2,0:T(8,128)(2,1)} %bitcast.60), kind=kOutput, calls=%fused_computation.15 | convolution fusion | flops 275775488 | bytes 1769472 | tf_op jit(solution)/shard_map/rhts,rshv->rthv/dot_general | solution.py:82
  104.9 63.5 %all-gather.3.cloned.1.call-done = bf16[12,4,273,112]{3,1,2,0:T(4,128)(2,1)} async-done(((bf16[3,4,273,112]{3,1,2,0:T(4,128)(2,1)}), bf16[12,4,273,112]{3,1,2,0:T(4,128)(2,1)}) %all-gather.3.cloned.1.call-update) | async-done | bytes 2935312 | tf_op jit(solution)/shard_map/all_gather | solution.py:65
  168.4 2.8 %fusion.6 = f32[1,4,273,112]{3,0,2,1:T(1,128)S(1)} fusion(bf16[12,4,273,112]{3,1,2,0:T(4,128)(2,1)} %all-gather.3.cloned.1.call-done, s32[]{:T(128)} %bitcast.52), kind=kOutput, calls=%fused_computation.7 | convolution fusion | flops 2935308 | bytes 3424516 | tf_op jit(solution)/shard_map/rp,phev->rhev/dot_general | solution.py:72
  171.2 1.3 multiply_reduce_fusion
  172.5 0.1 multiply_convert_fusion.3
  172.7 12.8 %all_gather.11 = bf16[1024,448]{0,1:T(8,128)(2,1)S(1)} all-gather(bf16[512,448]{0,1:T(8,128)(2,1)S(1)} %bitcast.56), channel_id=1, replica_groups=mesh['req'=4,'row'=4,'col'=2] {'col'}, dimensions={0}, use_global_device_ids=true | all-gather | bytes 1376256 | tf_op jit(solution)/shard_map/all_gather | solution.py:94
  185.5 2.5 %convert_bitcast_fusion = bf16[896,1024]{0,1:T(8,128)(2,1)} fusion(bf16[1024,448]{0,1:T(8,128)(2,1)S(1)} %all_gather.11, bf16[448,896]{1,0:T(8,128)(2,1)S(1)} %copy-done.4), kind=kOutput, calls=%fused_computation.12 | convolution fusion | flops 823001088 | bytes 3555328 | tf_op jit(solution)/shard_map/dot_general | solution.py:92
  188.1 0.2 copy.11
  188.3 28.6 %reduce-scatter.5.cloned.1.call-done = bf16[896,256]{0,1:T(8,128)(2,1)} async-done(((bf16[896,1024]{0,1:T(8,128)(2,1)}), bf16[896,256]{0,1:T(8,128)(2,1)}) %reduce-scatter.5.cloned.1.call-update) | async-done | bytes 458768 | tf_op jit(solution)/shard_map/reduce_scatter | solution.py:98
  216.9 1.1 add_convert_fusion
  218.0 1.0 copy.12
  (16 shorter events, 0.1 us)
Async XLA Ops:
  7.4 30.6 %copy-start = (bf16[896,576]{0,1:T(8,128)(2,1)S(1)}, bf16[896,576]{0,1:T(8,128)(2,1)}, u32[]{:S(2)}) copy-start(bf16[896,576]{0,1:T(8,128)(2,1)} %param.9) | copy-start | bytes 3096580
  7.4 30.6 %all-gather.5.cloned.1.call-start = ((), (), s32[]{:S(2)}) async-start(), calls=%async_computation.4 | async-start | bytes 2293760 | tf_op jit(solution)/shard_map/all_gather | solution.py:42
  8.1 67.9 %all-reduce.2.cloned.1.call-start = ((), (), s32[]{:S(2)}) async-start(), calls=%async_computation.2 | async-start | bytes 1677312 | tf_op jit(solution)/shard_map/psum | solution.py:64
  9.9 11.0 %copy-start.1 = (bf16[3,64,4096]{2,1,0:T(8,128)(2,1)S(1)}, bf16[3,64,4096]{2,1,0:T(8,128)(2,1)}, u32[]{:S(2)}) copy-start(bf16[3,64,4096]{2,1,0:T(8,128)(2,1)} %param.12) | copy-start | bytes 4718596
  37.9 39.5 %copy-start.3 = (f32[448]{0:T(512)S(1)}, f32[448]{0:T(512)}, u32[]{:S(2)}) copy-start(f32[448]{0:T(512)} %param.11) | copy-start | bytes 5380
  37.9 62.2 %reduce-scatter.3.cloned.1.call-start = ((), (), s32[]{:S(2)}) async-start(), calls=%async_computation.5 | async-start | bytes 1769472 | tf_op jit(solution)/shard_map/reduce_scatter | solution.py:47
  41.9 126.5 %all-gather.3.cloned.1.call-start = ((), (), s32[]{:S(2)}) async-start(), calls=%async_computation.3 | async-start | bytes 4193280 | tf_op jit(solution)/shard_map/all_gather | solution.py:65
  76.0 140.9 %reduce-scatter.5.cloned.1.call-start = ((), (), s32[]{:S(2)}) async-start(), calls=%async_computation.6 | async-start | bytes 2293760 | tf_op jit(solution)/shard_map/reduce_scatter | solution.py:98
  171.2 14.3 %copy-start.4 = (bf16[448,896]{1,0:T(8,128)(2,1)S(1)}, bf16[448,896]{1,0:T(8,128)(2,1)}, u32[]{:S(2)}) copy-start(bf16[448,896]{1,0:T(8,128)(2,1)} %param.10) | copy-start | bytes 2408452
  185.5 2.6 %copy-start.2 = (bf16[896,256]{1,0:T(8,128)(2,1)S(1)}, bf16[896,256]{1,0:T(8,128)(2,1)}, u32[]{:S(2)}) copy-start(bf16[896,256]{1,0:T(8,128)(2,1)} %param.8) | copy-start | bytes 1376260
Sparse Core Ops, SparseCore 0:
  9.7 24.0 all-gather.4
  188.2 28.6 reduce-scatter.4
Sparse Core Ops, SparseCore 1:
  38.0 38.0 all-reduce.1
  78.2 21.9 reduce-scatter.2
  101.6 66.8 all-gather.2
where the time goes:
time: 227 us
  waiting for transfers between devices  149 us (66%)
  matrix products  28.6 us (13%)
  other arithmetic  16.5 us (7%)
  between operations  16.5 us (7%)
  blocking collectives  12.8 us (6%)
  local copies, waits for them, and re-layouts  2.58 us (1%)
    all_gather x1, waiting for transfers between devices, shards(): lax.all_gather(summed_state.astype(jnp.bfloat16), 'req', axis=0, tiled=True)  63.5 us
    psum x1, waiting for transfers between devices, shards(): lax.psum(partial_state.astype(jnp.bfloat16), 'col').astype(jnp.float32)  34 us
    reduce_scatter x1, waiting for transfers between devices, shards(): lax.psum_scatter(out_terms.astype(jnp.bfloat16), 'row', scatter_dimension...  28.6 us
    reduce_scatter x1, waiting for transfers between devices, shards(): lax.psum_scatter(partial_proj.astype(jnp.bfloat16), 'col', scatter_dimens...  22.6 us
    dot_general x1, matrix products, shards(): jnp.einsum('phet,phvt->phev', feats_cached, values_cached, preferred_elem...  15.3 us
    all_gather x1, blocking collectives, shards(): lax.all_gather(normed, 'col', axis=0, tiled=True)  12.8 us
    another operation x3, other arithmetic  11.7 us
  transfers between devices with their start and end apart: 5, of which 4 were waited for; matrix products, arithmetic and copies ran while one was open for 17% of the time, Pallas kernels for 0%

commit v1 on v0

v1 whole, which is shorter than its diff:
```python
import functools

import jax
import jax.numpy as jnp
from jax import lax
from jax.experimental import pallas as pl
from jax.experimental.pallas import tpu as pltpu
from jax.sharding import PartitionSpec as P

FEAT = 16
SLOTS = 512
HD = 112
NF = 160
epsilon = 1e-05
MESH = pl.DeviceIdType.MESH
BF = jnp.bfloat16
F32 = jnp.float32


def products(u, linear, diag, cross, const):
    parts = [(u * linear).astype(BF), (u * u * diag).astype(BF)]
    left = u * cross
    for s in range(1, 8):
        rolled = jnp.concatenate([u[s:], u[:s]], axis=0)
        parts.append((left * rolled).astype(BF))
    last = jnp.concatenate([left[:8] * u[8:], jnp.full((8, u.shape[1]), const, F32)], axis=0)
    parts.append(last.astype(BF))
    return jnp.concatenate(parts, axis=0)


def body(dims, tok_ref, qkv_ref, wo_ref, gain_ref, keys_ref, vals_ref, len_ref, own_ref, out_ref,
         tok_all, wo_all, qkv_t, wo_t, keys_v, vals_v, own_part, send_part, recv_part, proj,
         st_part, st_recv, sel, sel_recv, own_all, nrm, hid,
         ld_k, ld_v, tok_s, tok_r, wo_s, wo_r, part_s, part_r, st_s, st_r, sel_s, sel_r, ow_s, ow_r,
         nrm_s, nrm_r, hid_s, hid_r):
    n_req, n_row, n_col = dims
    n_x = n_row // 2
    z, rho, y = lax.axis_index("req"), lax.axis_index("row"), lax.axis_index("col")
    x, c = rho // 2, rho % 2
    mate = x * 2 + (1 - c)
    heads = wo_ref.shape[0] // HD
    width = 2 * FEAT + HD
    tr = tok_ref.shape[1]
    halves = SLOTS // tr
    n_pref, _, t_len = keys_ref.shape

    loads = []
    for h in range(heads):
        a = pltpu.make_async_copy(keys_ref.at[:, pl.ds(h * FEAT, FEAT)], keys_v.at[h], ld_k.at[h])
        b = pltpu.make_async_copy(vals_ref.at[:, pl.ds(h * HD, HD)], vals_v.at[h], ld_v.at[h])
        a.start()
        b.start()
        loads.append((a, b))

    barrier = pltpu.get_barrier_semaphore()
    for d in range(1, n_row):
        pl.semaphore_signal(barrier, inc=1, device_id=(z, (rho + d) % n_row, y), device_id_type=MESH)
    for d in range(1, n_col):
        pl.semaphore_signal(barrier, inc=1, device_id=(z, rho, (y + d) % n_col), device_id_type=MESH)
    for d in range(1, n_req):
        pl.semaphore_signal(barrier, inc=1, device_id=((z + d) % n_req, rho, y), device_id_type=MESH)

    qkv_t[...] = qkv_ref[...].T
    pl.semaphore_wait(barrier, n_row + n_col + n_req - 3)

    def remote(src, dst, s, r, dev):
        return pltpu.make_async_remote_copy(src_ref=src, dst_ref=dst, send_sem=s, recv_sem=r,
                                            device_id=dev, device_id_type=MESH)

    sent = []

    def send(*args):
        copy = remote(*args)
        copy.start()
        sent.append(copy)

    def spread(src, dst, ss, rs):
        for d in range(1, n_x):
            send(src, dst.at[2 * d], ss.at[2 * d], rs.at[2 * d], (z, ((x + d) % n_x) * 2 + c, y))
        send(src, dst.at[1], ss.at[1], rs.at[1], (z, mate, y))

    def forward(dst, ss, rs, d):
        remote(dst.at[2 * d], dst.at[2 * d], ss.at[2 * d], rs.at[2 * d], (z, mate, y)).wait_recv()
        send(dst.at[2 * d], dst.at[2 * d + 1], ss.at[2 * d + 1], rs.at[2 * d + 1], (z, mate, y))

    def arrived(dst, ss, rs, slot):
        remote(dst.at[slot], dst.at[slot], ss.at[slot], rs.at[slot], (z, mate, y)).wait_recv()

    def slot_row(slot):
        d, s = slot // 2, slot % 2
        return ((x - d + n_x) % n_x) * 2 + (c if s == 0 else 1 - c)

    spread(tok_ref, tok_all, tok_s, tok_r)
    for d in range(1, n_req):
        send(own_ref, own_all.at[d], ow_s.at[d], ow_r.at[d], ((z + d) % n_req, rho, y))

    def part_copy(slot):
        row = slot_row(slot)
        g = row * tr // SLOTS
        j = row % halves
        d = (g - y + n_col) % n_col
        k = (d - 1 + n_col) % n_col
        return g, j, remote(send_part.at[slot], recv_part.at[k, j], part_s.at[slot], part_r.at[k, j], (z, rho, g))

    def project(slot):
        tokens = tok_ref[...] if slot == 0 else tok_all[slot]
        value = jnp.dot(qkv_t[...], tokens, preferred_element_type=F32).astype(BF)
        g, j, copy = part_copy(slot)

        @pl.when(g == y)
        def _():
            own_part[j] = value

        @pl.when(g != y)
        def _():
            send_part[slot] = value
            copy.start()

    project(0)
    arrived(tok_all, tok_s, tok_r, 1)
    project(1)
    spread(wo_ref, wo_all, wo_s, wo_r)

    step = min(1024, t_len)

    def state(h):
        loads[h][0].wait()
        loads[h][1].wait()

        def one(p, carry):
            total = jnp.zeros((HD, NF), F32)
            for t in range(0, t_len, step):
                u = keys_v[h, p, :, t:t + step].astype(F32)
                feats = products(u, 1.0, 1.0, 1.0, 1.0)
                total += lax.dot_general(vals_v[h, p, :, t:t + step], feats, (((1,), (1,)), ((), ())),
                                         preferred_element_type=F32)
            st_part[h, p] = total.astype(BF)
            return carry

        lax.fori_loop(0, n_pref, one, 0)
        for d in range(1, n_col):
            send(st_part.at[h], st_recv.at[d, h], st_s.at[d, h], st_r.at[d, h], (z, rho, (y + d) % n_col))

    def choose(h):
        if h == 0:
            for d in range(1, n_req):
                remote(own_ref, own_all.at[d], ow_s.at[d], ow_r.at[d], (z, rho, y)).wait_recv()
        for d in range(1, n_col):
            remote(st_part.at[h], st_recv.at[d, h], st_s.at[d, h], st_r.at[d, h], (z, rho, y)).wait_recv()
        sums = []
        for p in range(n_pref):
            total = st_part[h, p].astype(F32)
            for d in range(1, n_col):
                total += st_recv[d, h, p].astype(F32)
            sums.append(total)
        for d in list(range(1, n_req)) + [0]:
            k = (n_req - d) % n_req
            owner = own_ref[0:1, 0:NF] if k == 0 else own_all[k, 0:1, 0:NF]
            value = jnp.zeros((HD, NF), F32)
            for p in range(n_pref):
                value = jnp.where(owner == z * n_pref + p, sums[p], value)
            sel[d, h] = value.astype(BF)
            if d:
                send(sel.at[d, h], sel_recv.at[d, h], sel_s.at[d, h], sel_r.at[d, h], ((z + d) % n_req, rho, y))

    half = max(1, heads // 2)
    for h in range(heads):
        state(h)
        if h > 0:
            choose(h - 1)
        if h == half - 1:
            for d in range(1, n_x):
                forward(tok_all, tok_s, tok_r, d)
        if h == half:
            for d in range(1, n_x):
                project(2 * d)
                arrived(tok_all, tok_s, tok_r, 2 * d + 1)
                project(2 * d + 1)
    choose(heads - 1)
    for d in range(1, n_x):
        forward(wo_all, wo_s, wo_r, d)

    for j in range(halves):
        total = own_part[j].astype(F32)
        for d in range(1, n_col):
            k = d - 1
            remote(send_part.at[0], recv_part.at[k, j], part_s.at[0], part_r.at[k, j], (z, rho, y)).wait_recv()
            total += recv_part[k, j].astype(F32)
        proj[:, j * tr:(j + 1) * tr] = total.astype(BF)

    def hid_copy(d, h, j):
        row = ((y - d + n_col) % n_col) * halves + j
        cols = pl.ds(h * HD, HD)
        return row, remote(nrm.at[d, h, j], hid.at[rho, cols], hid_s.at[d, h, j], hid_r.at[rho, h], (z, row, y))

    def scatter(d, h):
        for j in range(halves):
            row, copy = hid_copy(d, h, j)

            @pl.when(row == rho)
            def _():
                hid[rho, h * HD:(h + 1) * HD] = nrm[d, h, j]

            @pl.when(row != rho)
            def _():
                copy.start()

    def pass_on(h):
        for d in range(1, n_col):
            remote(nrm.at[0, h], nrm.at[d, h], nrm_s.at[d, h], nrm_r.at[d, h], (z, rho, y)).wait_recv()
            scatter(d, h)

    tile = min(tr, 256)
    live = len_ref[0:1, :]
    for h in range(heads):
        base = h * width
        q = proj[base:base + FEAT].astype(F32)
        k_rows = proj[base + FEAT:base + 2 * FEAT].astype(F32).T.astype(BF)
        v = proj[base + 2 * FEAT:base + width]
        pos = lax.broadcasted_iota(jnp.int32, (HD, SLOTS), 1)
        active = pos < live
        v = jnp.where(active, v.astype(F32), 0.0).astype(BF)
        for d in range(1, n_req):
            remote(sel.at[d, h], sel_recv.at[d, h], sel_s.at[d, h], sel_r.at[d, h], (z, rho, y)).wait_recv()
        s_t = sel[0, h].astype(F32)
        for d in range(1, n_req):
            s_t += sel_recv[d, h].astype(F32)
        feats = products(q, 0.25, 1.0 / 32, 1.0 / 16, 0.125)
        carried = jnp.dot(s_t.astype(BF), feats, preferred_element_type=F32)
        for t in range(0, SLOTS, tile):
            keep = t + tile
            scores = jnp.dot(k_rows[:keep], q[:, t:keep].astype(BF), preferred_element_type=F32)
            weights = 1.0 + scores * 0.25 + scores * scores * (0.5 / FEAT)
            si = lax.broadcasted_iota(jnp.int32, (keep, tile), 0)
            ti = lax.broadcasted_iota(jnp.int32, (keep, tile), 1) + t
            weights = jnp.where(si <= ti, weights, 0.0).astype(BF)
            att = carried[:, t:keep] + jnp.dot(v[:, :keep], weights, preferred_element_type=F32)
            att = jnp.where(active[:, t:keep], att, 0.0)
            inv = lax.rsqrt(jnp.mean(att * att, axis=0, keepdims=True) + epsilon)
            normed = (att * inv * gain_ref[h * HD:(h + 1) * HD, :]).astype(BF)
            j, o = t // tr, t % tr
            nrm[0, h, j, :, o:o + tile] = normed
        for d in range(1, n_col):
            send(nrm.at[0, h], nrm.at[d, h], nrm_s.at[d, h], nrm_r.at[d, h], (z, rho, (y + d) % n_col))
        scatter(0, h)
        if h > 0:
            pass_on(h - 1)
    wo_t[0] = wo_ref[...].T
    pass_on(heads - 1)
    for slot in range(1, n_row):
        if slot == 1 or slot % 2:
            arrived(wo_all, wo_s, wo_r, slot)
        wo_t[slot] = wo_all[slot].T

    for k in range(1, n_row):
        src = (rho + k) % n_row
        for h in range(heads):
            cols = pl.ds(h * HD, HD)
            remote(nrm.at[0, h, 0], hid.at[src, cols], hid_s.at[0, h, 0], hid_r.at[src, h], (z, rho, y)).wait_recv()

    total = tok_ref[...].astype(F32)
    for slot in range(n_row):
        total += jnp.dot(wo_t[slot], hid[slot_row(slot)], preferred_element_type=F32)
    out_ref[...] = total.astype(BF)

    for copy in sent:
        copy.wait_send()
    for slot in range(n_row):
        g, _, copy = part_copy(slot)

        @pl.when(g != y)
        def _():
            copy.wait_send()
    for d in range(n_col):
        for h in range(heads):
            for j in range(halves):
                row, copy = hid_copy(d, h, j)

                @pl.when(row != rho)
                def _():
                    copy.wait_send()


def shards(dims, tokens, qkv_weight, out_weight, head_gain, prefix_keys, prefix_values, suffix_len, prefix_owner):
    n_req, n_row, n_col = dims
    dk, tr = tokens.shape
    rows, wide = out_weight.shape
    heads = rows // HD
    halves = SLOTS // tr
    qkv = qkv_weight.shape[1]
    n_pref, _, t_len = prefix_keys.shape
    lens = jnp.broadcast_to(suffix_len[:, None], (8, SLOTS))
    owners = jnp.broadcast_to(prefix_owner[:, None], (8, 256))
    vm = pltpu.VMEM
    dma = pltpu.SemaphoreType.DMA
    scratch = [
        vm((n_row, dk, tr), BF), vm((n_row, rows, wide), BF), vm((qkv, dk), BF), vm((n_row, wide, rows), BF),
        vm((heads, n_pref, FEAT, t_len), BF), vm((heads, n_pref, HD, t_len), BF),
        vm((halves, qkv, tr), BF), vm((n_row, qkv, tr), BF), vm((n_col, halves, qkv, tr), BF), vm((qkv, SLOTS), BF),
        vm((heads, n_pref, HD, NF), BF), vm((n_col, heads, n_pref, HD, NF), BF),
        vm((n_req, heads, HD, NF), BF), vm((n_req, heads, HD, NF), BF), vm((n_req, 8, 256), jnp.int32),
        vm((n_col, heads, halves, HD, tr), BF), vm((n_row, rows, tr), BF),
        dma((heads,)), dma((heads,)), dma((n_row,)), dma((n_row,)), dma((n_row,)), dma((n_row,)),
        dma((n_row,)), dma((n_col, halves)), dma((n_col, heads)), dma((n_col, heads)),
        dma((n_req, heads)), dma((n_req, heads)), dma((n_req,)), dma((n_req,)),
        dma((n_col, heads)), dma((n_col, heads)), dma((n_col, heads, halves)), dma((n_row, heads)),
    ]
    here = pl.BlockSpec(memory_space=pltpu.VMEM)
    far = pl.BlockSpec(memory_space=pl.ANY)
    return pl.pallas_call(
        functools.partial(body, dims),
        out_shape=jax.ShapeDtypeStruct(tokens.shape, BF),
        in_specs=[here, here, here, here, far, far, here, here],
        out_specs=here,
        scratch_shapes=scratch,
        compiler_params=pltpu.CompilerParams(collective_id=0, has_side_effects=True,
                                             vmem_limit_bytes=60 * 1024 * 1024),
    )(tokens, qkv_weight, out_weight, head_gain[:, None], prefix_keys, prefix_values, lens, owners)


def solution(mesh):
    in_specs = (
        P("col", ("req", "row")),
        P("col", "row"),
        P("row", "col"),
        P("row"),
        P("req", "row", "col"),
        P("req", "row", "col"),
        P(("req", "col")),
        P(("req", "col")),
    )
    out_specs = P("col", ("req", "row"))
    dims = (mesh.shape["req"], mesh.shape["row"], mesh.shape["col"])
    return jax.shard_map(functools.partial(shards, dims), mesh=mesh, in_specs=in_specs, out_specs=out_specs,
                         check_vma=False)
```

time: 227 us -> 75.2 us (0.33)
  waiting for transfers between devices: 149 us -> 0 us
  Pallas kernels: 0 us -> 66 us
  matrix products: 28.6 us -> 0 us
  other arithmetic: 16.5 us -> 0 us
  between operations: 16.5 us -> 1.31 us
  blocking collectives: 12.8 us -> 0 us
  local copies, waits for them, and re-layouts: 2.58 us -> 6.86 us
    pallas_call x0 -> x1, Pallas kernels: none -> 66 us  [shards(): pl.pallas_call(functools.partial(body, dims), out_shape=jax.ShapeDtypeStr...]
    all_gather x2 -> x0, waiting for transfers between devices: 63.5 us -> none  [the longest x1 63.5 us: shards(): lax.all_gather(summed_state.astype(jnp.bfloat16), 'req', axis=0, tiled=True)]
    reduce_scatter x2 -> x0, waiting for transfers between devices: 51.2 us -> none  [the longest x1 28.6 us: shards(): lax.psum_scatter(out_terms.astype(jnp.bfloat16), 'row', scatter_dimension...]
    psum x1 -> x0, waiting for transfers between devices: 34 us -> none  [shards(): lax.psum(partial_state.astype(jnp.bfloat16), 'col').astype(jnp.float32)]
    dot_general x6 -> x0, matrix products: 28.6 us -> none  [the longest x1 15.3 us: shards(): jnp.einsum('phet,phvt->phev', feats_cached, values_cached, preferred_elem...]
    all_gather x1 -> x0, blocking collectives: 12.8 us -> none  [shards(): lax.all_gather(normed, 'col', axis=0, tiled=True)]
    another operation x3 -> x0, other arithmetic: 11.7 us -> none
    unnamed x11 -> x2, local copies, waits for them, and re-layouts: 0.27 us -> 4.16 us
  transfers between devices with their start and end apart: 5 -> 0, of which waited for: 4 -> 0; matrix products, arithmetic and copies ran while one was open for 17% -> 0% of each run, Pallas kernels for 0% -> 0%
where the time goes in v1:
time: 75.2 us; the launch traced here: 74.2 us
  Pallas kernels  66 us (88%)
  local copies, waits for them, and re-layouts  6.86 us (9%)
  between operations  1.31 us (2%)
    pallas_call x1, Pallas kernels, shards(): pl.pallas_call(functools.partial(body, dims), out_shape=jax.ShapeDtypeStr...  66 us
    unnamed x2, local copies, waits for them, and re-layouts  4.16 us
    broadcast_in_dim x1, local copies, waits for them, and re-layouts, shards(): head_gain[:, None]  1.51 us

profile of v1, /device:TPU:0, one launch (start us, length us, event | category | flops | bytes accessed | tf_op | source)
XLA Modules:
  0.0 74.2 jit_solution(4490049077367117806)
XLA Ops:
  1.3 0.6 broadcast_in_dim.23.own_ref
  1.9 0.6 broadcast_in_dim.21.len_ref
  2.5 1.5 %copy.11.gain_ref = f32[448,1]{1,0:T(8,128)} copy(f32[448,1]{0,1:T(1,128)} %bitcast.5) | data formatting | bytes 3584 | tf_op jit(solution)/shard_map/broadcast_in_dim | solution.py:318
  4.0 2.3 %copy.10.qkv_ref = bf16[896,576]{1,0:T(8,128)(2,1)} copy(bf16[896,576]{0,1:T(8,128)(2,1)} %param.9) | data formatting | bytes 2064384 | tf_op args[1]
  6.3 66.0 %shard_map.82 = bf16[896,256]{1,0:T(8,128)(2,1)} custom-call(bf16[896,256]{1,0:T(8,128)(2,1)} %tok_ref.1, bf16[896,576]{1,0:T(8,128)(2,1)} %copy.10.qkv_ref, bf16[448,896]{1,0:T(8,128)(2,1)} %wo_ref.1, f32[448,1]{1,0:T(8,128)} %copy.11.gain_ref, bf16[3,64,4096]{2,1,0:T(8,128)(2,1)} %keys_ref.1, bf16[3,448,4096]{2,1,0:T(8,128)(2,1)} %vals_ref.1, ...), custom_call_target="tpu_custom_call" | custom-call | tf_op jit(solution)/shard_map/pallas_call | solution.py:310
  72.4 1.8 %copy.15 = bf16[896,256]{1,0:T(8,128)(2,1)} copy(bf16[896,256]{1,0:T(8,128)(2,1)} %shard_map.82) | data formatting | bytes 917504

commit v2 on v1

--- a/solution.py
+++ b/solution.py
@@ -28,10 +28,10 @@
     return jnp.concatenate(parts, axis=0)
 
 
-def body(dims, tok_ref, qkv_ref, wo_ref, gain_ref, keys_ref, vals_ref, len_ref, own_ref, out_ref,
-         tok_all, wo_all, qkv_t, wo_t, keys_v, vals_v, own_part, send_part, recv_part, proj,
+def body(dims, tok_any, qkv_any, wo_any, gain_ref, keys_ref, vals_ref, len_ref, own_ref, out_ref,
+         tok_ref, wo_ref, gain_c, inner, tok_all, wo_all, qkv_t, wo_t, keys_v, vals_v, own_part, send_part, recv_part, proj,
          st_part, st_recv, sel, sel_recv, own_all, nrm, hid,
-         ld_k, ld_v, tok_s, tok_r, wo_s, wo_r, part_s, part_r, st_s, st_r, sel_s, sel_r, ow_s, ow_r,
+         ld_w, ld_k, ld_v, tok_s, tok_r, wo_s, wo_r, part_s, part_r, st_s, st_r, sel_s, sel_r, ow_s, ow_r,
          nrm_s, nrm_r, hid_s, hid_r):
     n_req, n_row, n_col = dims
     n_x = n_row // 2
@@ -44,6 +44,11 @@
     halves = SLOTS // tr
     n_pref, _, t_len = keys_ref.shape
 
+    first = [pltpu.make_async_copy(tok_any, tok_ref, ld_w.at[0]),
+             pltpu.make_async_copy(qkv_any, qkv_t, ld_w.at[1]),
+             pltpu.make_async_copy(wo_any, wo_ref, ld_w.at[2])]
+    first[0].start()
+    first[1].start()
     loads = []
     for h in range(heads):
         a = pltpu.make_async_copy(keys_ref.at[:, pl.ds(h * FEAT, FEAT)], keys_v.at[h], ld_k.at[h])
@@ -51,6 +56,7 @@
         a.start()
         b.start()
         loads.append((a, b))
+    first[2].start()
 
     barrier = pltpu.get_barrier_semaphore()
     for d in range(1, n_row):
@@ -60,7 +66,9 @@
     for d in range(1, n_req):
         pl.semaphore_signal(barrier, inc=1, device_id=((z + d) % n_req, rho, y), device_id_type=MESH)
 
-    qkv_t[...] = qkv_ref[...].T
+    own_all[0] = jnp.full((8, 128), own_ref[0], jnp.int32)
+    gain_c[...] = jnp.broadcast_to(gain_ref[...], (8, gain_ref.shape[1])).T
+    first[0].wait()
     pl.semaphore_wait(barrier, n_row + n_col + n_req - 3)
 
     def remote(src, dst, s, r, dev):
@@ -92,7 +100,7 @@
 
     spread(tok_ref, tok_all, tok_s, tok_r)
     for d in range(1, n_req):
-        send(own_ref, own_all.at[d], ow_s.at[d], ow_r.at[d], ((z + d) % n_req, rho, y))
+        send(own_all.at[0], own_all.at[d], ow_s.at[d], ow_r.at[d], ((z + d) % n_req, rho, y))
 
     def part_copy(slot):
         row = slot_row(slot)
@@ -116,10 +124,10 @@
             send_part[slot] = value
             copy.start()
 
+    first[1].wait()
     project(0)
     arrived(tok_all, tok_s, tok_r, 1)
     project(1)
-    spread(wo_ref, wo_all, wo_s, wo_r)
 
     step = min(1024, t_len)
 
@@ -128,11 +136,11 @@
         loads[h][1].wait()
 
         def one(p, carry):
-            total = jnp.zeros((HD, NF), F32)
+            total = jnp.zeros((NF, HD), F32)
             for t in range(0, t_len, step):
                 u = keys_v[h, p, :, t:t + step].astype(F32)
                 feats = products(u, 1.0, 1.0, 1.0, 1.0)
-                total += lax.dot_general(vals_v[h, p, :, t:t + step], feats, (((1,), (1,)), ((), ())),
+                total += lax.dot_general(feats, vals_v[h, p, :, t:t + step], (((1,), (1,)), ((), ())),
                                          preferred_element_type=F32)
             st_part[h, p] = total.astype(BF)
             return carry
@@ -144,7 +152,7 @@
     def choose(h):
         if h == 0:
             for d in range(1, n_req):
-                remote(own_ref, own_all.at[d], ow_s.at[d], ow_r.at[d], (z, rho, y)).wait_recv()
+                remote(own_all.at[0], own_all.at[d], ow_s.at[d], ow_r.at[d], (z, rho, y)).wait_recv()
         for d in range(1, n_col):
             remote(st_part.at[h], st_recv.at[d, h], st_s.at[d, h], st_r.at[d, h], (z, rho, y)).wait_recv()
         sums = []
@@ -155,8 +163,8 @@
             sums.append(total)
         for d in list(range(1, n_req)) + [0]:
             k = (n_req - d) % n_req
-            owner = own_ref[0:1, 0:NF] if k == 0 else own_all[k, 0:1, 0:NF]
-            value = jnp.zeros((HD, NF), F32)
+            owner = own_all[k, 0:1, 0:HD]
+            value = jnp.zeros((NF, HD), F32)
             for p in range(n_pref):
                 value = jnp.where(owner == z * n_pref + p, sums[p], value)
             sel[d, h] = value.astype(BF)
@@ -168,17 +176,18 @@
         state(h)
         if h > 0:
             choose(h - 1)
-        if h == half - 1:
+        if h == half:
             for d in range(1, n_x):
                 forward(tok_all, tok_s, tok_r, d)
-        if h == half:
+                project(2 * d)
+            first[2].wait()
+            spread(wo_ref, wo_all, wo_s, wo_r)
+        if h == heads - 1:
             for d in range(1, n_x):
-                project(2 * d)
                 arrived(tok_all, tok_s, tok_r, 2 * d + 1)
                 project(2 * d + 1)
     choose(heads - 1)
-    for d in range(1, n_x):
-        forward(wo_all, wo_s, wo_r, d)
+    wo_t[0] = wo_ref[...].T
 
     for j in range(halves):
         total = own_part[j].astype(F32)
@@ -211,57 +220,58 @@
             scatter(d, h)
 
     tile = min(tr, 256)
-    live = len_ref[0:1, :]
+    live = len_ref[0]
+    active = lax.broadcasted_iota(jnp.int32, (HD, SLOTS), 1) < live
     for h in range(heads):
         base = h * width
-        q = proj[base:base + FEAT].astype(F32)
+        q = proj[base:base + FEAT]
         k_rows = proj[base + FEAT:base + 2 * FEAT].astype(F32).T.astype(BF)
         v = proj[base + 2 * FEAT:base + width]
-        pos = lax.broadcasted_iota(jnp.int32, (HD, SLOTS), 1)
-        active = pos < live
         v = jnp.where(active, v.astype(F32), 0.0).astype(BF)
-        for d in range(1, n_req):
-            remote(sel.at[d, h], sel_recv.at[d, h], sel_s.at[d, h], sel_r.at[d, h], (z, rho, y)).wait_recv()
-        s_t = sel[0, h].astype(F32)
-        for d in range(1, n_req):
-            s_t += sel_recv[d, h].astype(F32)
-        feats = products(q, 0.25, 1.0 / 32, 1.0 / 16, 0.125)
-        carried = jnp.dot(s_t.astype(BF), feats, preferred_element_type=F32)
         for t in range(0, SLOTS, tile):
             keep = t + tile
-            scores = jnp.dot(k_rows[:keep], q[:, t:keep].astype(BF), preferred_element_type=F32)
+            scores = jnp.dot(k_rows[:keep], q[:, t:keep], preferred_element_type=F32)
             weights = 1.0 + scores * 0.25 + scores * scores * (0.5 / FEAT)
             si = lax.broadcasted_iota(jnp.int32, (keep, tile), 0)
             ti = lax.broadcasted_iota(jnp.int32, (keep, tile), 1) + t
             weights = jnp.where(si <= ti, weights, 0.0).astype(BF)
-            att = carried[:, t:keep] + jnp.dot(v[:, :keep], weights, preferred_element_type=F32)
-            att = jnp.where(active[:, t:keep], att, 0.0)
-            inv = lax.rsqrt(jnp.mean(att * att, axis=0, keepdims=True) + epsilon)
-            normed = (att * inv * gain_ref[h * HD:(h + 1) * HD, :]).astype(BF)
-            j, o = t // tr, t % tr
-            nrm[0, h, j, :, o:o + tile] = normed
+            inner[h, :, t:keep] = jnp.dot(v[:, :keep], weights, preferred_element_type=F32)
+
+    for d in range(1, n_x):
+        forward(wo_all, wo_s, wo_r, d)
+
+    for h in range(heads):
+        feats = products(proj[h * width:h * width + FEAT].astype(F32), 0.25, 1.0 / 32, 1.0 / 16, 0.125)
+        for d in range(1, n_req):
+            remote(sel.at[d, h], sel_recv.at[d, h], sel_s.at[d, h], sel_r.at[d, h], (z, rho, y)).wait_recv()
+        state_h = sel[0, h].astype(F32)
+        for d in range(1, n_req):
+            state_h += sel_recv[d, h].astype(F32)
+        att = inner[h] + jnp.dot(state_h.T.astype(BF), feats, preferred_element_type=F32)
+        att = jnp.where(active, att, 0.0)
+        inv = lax.rsqrt(jnp.mean(att * att, axis=0, keepdims=True) + epsilon)
+        normed = (att * inv * gain_c[h * HD:(h + 1) * HD, 0:1]).astype(BF)
+        for j in range(halves):
+            nrm[0, h, j] = normed[:, j * tr:(j + 1) * tr]
         for d in range(1, n_col):
             send(nrm.at[0, h], nrm.at[d, h], nrm_s.at[d, h], nrm_r.at[d, h], (z, rho, (y + d) % n_col))
         scatter(0, h)
         if h > 0:
             pass_on(h - 1)
-    wo_t[0] = wo_ref[...].T
     pass_on(heads - 1)
     for slot in range(1, n_row):
         if slot == 1 or slot % 2:
             arrived(wo_all, wo_s, wo_r, slot)
         wo_t[slot] = wo_all[slot].T
 
-    for k in range(1, n_row):
-        src = (rho + k) % n_row
+    total = jnp.dot(wo_t[0], hid[rho], preferred_element_type=F32)
+    for slot in range(1, n_row):
+        src = slot_row(slot)
         for h in range(heads):
             cols = pl.ds(h * HD, HD)
             remote(nrm.at[0, h, 0], hid.at[src, cols], hid_s.at[0, h, 0], hid_r.at[src, h], (z, rho, y)).wait_recv()
-
-    total = tok_ref[...].astype(F32)
-    for slot in range(n_row):
-        total += jnp.dot(wo_t[slot], hid[slot_row(slot)], preferred_element_type=F32)
-    out_ref[...] = total.astype(BF)
+        total += jnp.dot(wo_t[slot], hid[src], preferred_element_type=F32)
+    out_ref[...] = total
 
     for copy in sent:
         copy.wait_send()
@@ -289,33 +299,34 @@
     halves = SLOTS // tr
     qkv = qkv_weight.shape[1]
     n_pref, _, t_len = prefix_keys.shape
-    lens = jnp.broadcast_to(suffix_len[:, None], (8, SLOTS))
-    owners = jnp.broadcast_to(prefix_owner[:, None], (8, 256))
     vm = pltpu.VMEM
     dma = pltpu.SemaphoreType.DMA
     scratch = [
+        vm((dk, tr), BF), vm((rows, wide), BF), vm((rows, 8), F32), vm((heads, HD, SLOTS), F32),
         vm((n_row, dk, tr), BF), vm((n_row, rows, wide), BF), vm((qkv, dk), BF), vm((n_row, wide, rows), BF),
         vm((heads, n_pref, FEAT, t_len), BF), vm((heads, n_pref, HD, t_len), BF),
         vm((halves, qkv, tr), BF), vm((n_row, qkv, tr), BF), vm((n_col, halves, qkv, tr), BF), vm((qkv, SLOTS), BF),
-        vm((heads, n_pref, HD, NF), BF), vm((n_col, heads, n_pref, HD, NF), BF),
-        vm((n_req, heads, HD, NF), BF), vm((n_req, heads, HD, NF), BF), vm((n_req, 8, 256), jnp.int32),
+        vm((heads, n_pref, NF, HD), BF), vm((n_col, heads, n_pref, NF, HD), BF),
+        vm((n_req, heads, NF, HD), BF), vm((n_req, heads, NF, HD), BF), vm((n_req, 8, 128), jnp.int32),
         vm((n_col, heads, halves, HD, tr), BF), vm((n_row, rows, tr), BF),
-        dma((heads,)), dma((heads,)), dma((n_row,)), dma((n_row,)), dma((n_row,)), dma((n_row,)),
+        dma((3,)), dma((heads,)), dma((heads,)), dma((n_row,)), dma((n_row,)), dma((n_row,)), dma((n_row,)),
         dma((n_row,)), dma((n_col, halves)), dma((n_col, heads)), dma((n_col, heads)),
         dma((n_req, heads)), dma((n_req, heads)), dma((n_req,)), dma((n_req,)),
         dma((n_col, heads)), dma((n_col, heads)), dma((n_col, heads, halves)), dma((n_row, heads)),
     ]
     here = pl.BlockSpec(memory_space=pltpu.VMEM)
     far = pl.BlockSpec(memory_space=pl.ANY)
-    return pl.pallas_call(
+    scalar = pl.BlockSpec(memory_space=pltpu.SMEM)
+    mixed = pl.pallas_call(
         functools.partial(body, dims),
-        out_shape=jax.ShapeDtypeStruct(tokens.shape, BF),
-        in_specs=[here, here, here, here, far, far, here, here],
+        out_shape=jax.ShapeDtypeStruct(tokens.shape, F32),
+        in_specs=[far, far, far, here, far, far, scalar, scalar],
         out_specs=here,
         scratch_shapes=scratch,
         compiler_params=pltpu.CompilerParams(collective_id=0, has_side_effects=True,
                                              vmem_limit_bytes=60 * 1024 * 1024),
-    )(tokens, qkv_weight, out_weight, head_gain[:, None], prefix_keys, prefix_values, lens, owners)
+    )(tokens, qkv_weight.T, out_weight, head_gain[None, :], prefix_keys, prefix_values, suffix_len, prefix_owner)
+    return (tokens.astype(F32) + mixed).astype(BF)
 
 
 def solution(mesh):

time: 75.2 us -> 65.9 us (0.88)
  local copies, waits for them, and re-layouts: 6.86 us -> 0.01 us
  Pallas kernels: 66 us -> 61.8 us
  other arithmetic: 0 us -> 2.04 us
    pallas_call x1, Pallas kernels: 66 us -> 61.8 us  [shards(): pl.pallas_call(functools.partial(body, dims), out_shape=jax.ShapeDtypeStr...]
    unnamed x2, local copies, waits for them, and re-layouts: 4.16 us -> 0.01 us
    broadcast_in_dim x3 -> x0, local copies, waits for them, and re-layouts: 2.7 us -> none  [the longest x1 1.51 us: shards(): head_gain[:, None]]
    convert_element_type x0 -> x1, other arithmetic: none -> 2.04 us  [shards(): return (tokens.astype(F32) + mixed).astype(BF)]
where the time goes in v2:
time: 65.9 us; the launch traced here: 65.2 us
  Pallas kernels  61.8 us (94%)
  other arithmetic  2.04 us (3%)
  between operations  1.37 us (2%)
    pallas_call x1, Pallas kernels, shards(): pl.pallas_call(functools.partial(body, dims), out_shape=jax.ShapeDtypeStr...  61.8 us
    convert_element_type x1, other arithmetic, shards(): return (tokens.astype(F32) + mixed).astype(BF)  2.04 us

profile of v2, /device:TPU:0, one launch (start us, length us, event | category | flops | bytes accessed | tf_op | source)
XLA Modules:
  0.0 65.2 jit_solution(7115172018884777445)
XLA Ops:
  0.0 0.0 copy-start
  1.4 61.8 %shard_map.82 = f32[896,256]{1,0:T(8,128)} custom-call(bf16[896,256]{1,0:T(8,128)(2,1)} %tok_any.1, bf16[576,896]{1,0:T(8,128)(2,1)} %bitcast.2, bf16[448,896]{1,0:T(8,128)(2,1)} %wo_any.1, f32[1,448]{1,0:T(1,128)} %bitcast.3, bf16[3,64,4096]{2,1,0:T(8,128)(2,1)} %keys_ref.1, bf16[3,448,4096]{2,1,0:T(8,128)(2,1)} %vals_ref.1, s32[1]{0:T(128)S(6)} %copy.9.len_ref, ...), custom_call_target="tpu_custom_call" | custom-call | tf_op jit(solution)/shard_map/pallas_call | solution.py:320
  63.2 0.0 copy-done
  63.2 2.0 %add_convert_fusion = bf16[896,256]{1,0:T(8,128)(2,1)} fusion(f32[896,256]{1,0:T(8,128)} %shard_map.82, bf16[896,256]{1,0:T(8,128)(2,1)S(1)} %copy-done), kind=kLoop, calls=%fused_computation | loop fusion | flops 688128 | bytes 1835008 | tf_op jit(solution)/shard_map/convert_element_type | solution.py:329
Async XLA Ops:
  0.0 63.2 %copy-start = (bf16[896,256]{1,0:T(8,128)(2,1)S(1)}, bf16[896,256]{1,0:T(8,128)(2,1)}, u32[]{:S(2)}) copy-start(bf16[896,256]{1,0:T(8,128)(2,1)} %tok_any.1) | copy-start | bytes 1376260

commit v3 on v2

--- a/solution.py
+++ b/solution.py
@@ -21,9 +21,18 @@
     parts = [(u * linear).astype(BF), (u * u * diag).astype(BF)]
     left = u * cross
     for s in range(1, 8):
-        rolled = jnp.concatenate([u[s:], u[:s]], axis=0)
-        parts.append((left * rolled).astype(BF))
+        parts.append((left * pltpu.roll(u, s, 0)).astype(BF))
     last = jnp.concatenate([left[:8] * u[8:], jnp.full((8, u.shape[1]), const, F32)], axis=0)
+    parts.append(last.astype(BF))
+    return jnp.concatenate(parts, axis=0)
+
+
+def key_products(rows):
+    u = rows.astype(F32)
+    parts = [rows, rows * rows]
+    for s in range(1, 8):
+        parts.append(rows * pltpu.roll(u, s, 0).astype(BF))
+    last = jnp.concatenate([u[:8] * u[8:], jnp.full((8, u.shape[1]), 1.0, F32)], axis=0)
     parts.append(last.astype(BF))
     return jnp.concatenate(parts, axis=0)
 
@@ -49,6 +58,7 @@
              pltpu.make_async_copy(wo_any, wo_ref, ld_w.at[2])]
     first[0].start()
     first[1].start()
+    first[2].start()
     loads = []
     for h in range(heads):
         a = pltpu.make_async_copy(keys_ref.at[:, pl.ds(h * FEAT, FEAT)], keys_v.at[h], ld_k.at[h])
@@ -56,7 +66,6 @@
         a.start()
         b.start()
         loads.append((a, b))
-    first[2].start()
 
     barrier = pltpu.get_barrier_semaphore()
     for d in range(1, n_row):
@@ -68,6 +77,8 @@
 
     own_all[0] = jnp.full((8, 128), own_ref[0], jnp.int32)
     gain_c[...] = jnp.broadcast_to(gain_ref[...], (8, gain_ref.shape[1])).T
+    first[2].wait()
+    wo_t[...] = wo_ref[...].T
     first[0].wait()
     pl.semaphore_wait(barrier, n_row + n_col + n_req - 3)
 
@@ -138,8 +149,7 @@
         def one(p, carry):
             total = jnp.zeros((NF, HD), F32)
             for t in range(0, t_len, step):
-                u = keys_v[h, p, :, t:t + step].astype(F32)
-                feats = products(u, 1.0, 1.0, 1.0, 1.0)
+                feats = key_products(keys_v[h, p, :, t:t + step])
                 total += lax.dot_general(feats, vals_v[h, p, :, t:t + step], (((1,), (1,)), ((), ())),
                                          preferred_element_type=F32)
             st_part[h, p] = total.astype(BF)
@@ -180,15 +190,12 @@
             for d in range(1, n_x):
                 forward(tok_all, tok_s, tok_r, d)
                 project(2 * d)
-            first[2].wait()
-            spread(wo_ref, wo_all, wo_s, wo_r)
+            spread(wo_t, wo_all, wo_s, wo_r)
         if h == heads - 1:
             for d in range(1, n_x):
                 arrived(tok_all, tok_s, tok_r, 2 * d + 1)
                 project(2 * d + 1)
     choose(heads - 1)
-    wo_t[0] = wo_ref[...].T
-
     for j in range(halves):
         total = own_part[j].astype(F32)
         for d in range(1, n_col):
@@ -259,18 +266,15 @@
         if h > 0:
             pass_on(h - 1)
     pass_on(heads - 1)
-    for slot in range(1, n_row):
-        if slot == 1 or slot % 2:
-            arrived(wo_all, wo_s, wo_r, slot)
-        wo_t[slot] = wo_all[slot].T
-
-    total = jnp.dot(wo_t[0], hid[rho], preferred_element_type=F32)
+    total = jnp.dot(wo_t[...], hid[rho], preferred_element_type=F32)
     for slot in range(1, n_row):
         src = slot_row(slot)
+        if slot % 2:
+            arrived(wo_all, wo_s, wo_r, slot)
         for h in range(heads):
             cols = pl.ds(h * HD, HD)
             remote(nrm.at[0, h, 0], hid.at[src, cols], hid_s.at[0, h, 0], hid_r.at[src, h], (z, rho, y)).wait_recv()
-        total += jnp.dot(wo_t[slot], hid[src], preferred_element_type=F32)
+        total += jnp.dot(wo_all[slot], hid[src], preferred_element_type=F32)
     out_ref[...] = total
 
     for copy in sent:
@@ -303,7 +307,7 @@
     dma = pltpu.SemaphoreType.DMA
     scratch = [
         vm((dk, tr), BF), vm((rows, wide), BF), vm((rows, 8), F32), vm((heads, HD, SLOTS), F32),
-        vm((n_row, dk, tr), BF), vm((n_row, rows, wide), BF), vm((qkv, dk), BF), vm((n_row, wide, rows), BF),
+        vm((n_row, dk, tr), BF), vm((n_row, wide, rows), BF), vm((qkv, dk), BF), vm((wide, rows), BF),
         vm((heads, n_pref, FEAT, t_len), BF), vm((heads, n_pref, HD, t_len), BF),
         vm((halves, qkv, tr), BF), vm((n_row, qkv, tr), BF), vm((n_col, halves, qkv, tr), BF), vm((qkv, SLOTS), BF),
         vm((heads, n_pref, NF, HD), BF), vm((n_col, heads, n_pref, NF, HD), BF),

time: 65.9 us -> 68.2 us (1.035)
  Pallas kernels: 61.8 us -> 64.2 us
    pallas_call x1, Pallas kernels: 61.8 us -> 64.2 us  [shards(): pl.pallas_call(functools.partial(body, dims), out_shape=jax.ShapeDtypeStr...]
where the time goes in v3:
time: 68.2 us; the launch traced here: 67.6 us
  Pallas kernels  64.2 us (94%)
  other arithmetic  2.04 us (3%)
  between operations  1.37 us (2%)
    pallas_call x1, Pallas kernels, shards(): pl.pallas_call(functools.partial(body, dims), out_shape=jax.ShapeDtypeStr...  64.2 us
    convert_element_type x1, other arithmetic, shards(): return (tokens.astype(F32) + mixed).astype(BF)  2.04 us

profile of v3, /device:TPU:0, one launch (start us, length us, event | category | flops | bytes accessed | tf_op | source)
XLA Modules:
  0.0 67.6 jit_solution(6617888148596118887)
XLA Ops:
  0.0 0.0 copy-start
  1.4 64.2 %shard_map.82 = f32[896,256]{1,0:T(8,128)} custom-call(bf16[896,256]{1,0:T(8,128)(2,1)} %tok_any.1, bf16[576,896]{1,0:T(8,128)(2,1)} %bitcast.2, bf16[448,896]{1,0:T(8,128)(2,1)} %wo_any.1, f32[1,448]{1,0:T(1,128)} %bitcast.3, bf16[3,64,4096]{2,1,0:T(8,128)(2,1)} %keys_ref.1, bf16[3,448,4096]{2,1,0:T(8,128)(2,1)} %vals_ref.1, s32[1]{0:T(128)S(6)} %copy.9.len_ref, ...), custom_call_target="tpu_custom_call" | custom-call | tf_op jit(solution)/shard_map/pallas_call | solution.py:324
  65.5 0.0 copy-done
  65.6 2.0 %add_convert_fusion = bf16[896,256]{1,0:T(8,128)(2,1)} fusion(f32[896,256]{1,0:T(8,128)} %shard_map.82, bf16[896,256]{1,0:T(8,128)(2,1)S(1)} %copy-done), kind=kLoop, calls=%fused_computation | loop fusion | flops 688128 | bytes 1835008 | tf_op jit(solution)/shard_map/convert_element_type | solution.py:333
Async XLA Ops:
  0.0 65.5 %copy-start = (bf16[896,256]{1,0:T(8,128)(2,1)S(1)}, bf16[896,256]{1,0:T(8,128)(2,1)}, u32[]{:S(2)}) copy-start(bf16[896,256]{1,0:T(8,128)(2,1)} %tok_any.1) | copy-start | bytes 1376260

commit v4 on v3

--- a/solution.py
+++ b/solution.py
@@ -47,7 +47,9 @@
     z, rho, y = lax.axis_index("req"), lax.axis_index("row"), lax.axis_index("col")
     x, c = rho // 2, rho % 2
     mate = x * 2 + (1 - c)
-    heads = wo_ref.shape[0] // HD
+    heads = gain_c.shape[0] // HD
+    b = z % 2
+    z_mate = z - b + 1 - b
     width = 2 * FEAT + HD
     tr = tok_ref.shape[1]
     halves = SLOTS // tr
@@ -61,11 +63,11 @@
     first[2].start()
     loads = []
     for h in range(heads):
-        a = pltpu.make_async_copy(keys_ref.at[:, pl.ds(h * FEAT, FEAT)], keys_v.at[h], ld_k.at[h])
-        b = pltpu.make_async_copy(vals_ref.at[:, pl.ds(h * HD, HD)], vals_v.at[h], ld_v.at[h])
-        a.start()
-        b.start()
-        loads.append((a, b))
+        pair = (pltpu.make_async_copy(keys_ref.at[:, pl.ds(h * FEAT, FEAT)], keys_v.at[h], ld_k.at[h]),
+                pltpu.make_async_copy(vals_ref.at[:, pl.ds(h * HD, HD)], vals_v.at[h], ld_v.at[h]))
+        pair[0].start()
+        pair[1].start()
+        loads.append(pair)
 
     barrier = pltpu.get_barrier_semaphore()
     for d in range(1, n_row):
@@ -78,7 +80,6 @@
     own_all[0] = jnp.full((8, 128), own_ref[0], jnp.int32)
     gain_c[...] = jnp.broadcast_to(gain_ref[...], (8, gain_ref.shape[1])).T
     first[2].wait()
-    wo_t[...] = wo_ref[...].T
     first[0].wait()
     pl.semaphore_wait(barrier, n_row + n_col + n_req - 3)
 
@@ -93,15 +94,22 @@
         copy.start()
         sent.append(copy)
 
-    def spread(src, dst, ss, rs):
-        for d in range(1, n_x):
-            send(src, dst.at[2 * d], ss.at[2 * d], rs.at[2 * d], (z, ((x + d) % n_x) * 2 + c, y))
-        send(src, dst.at[1], ss.at[1], rs.at[1], (z, mate, y))
-
     def forward(dst, ss, rs, d):
         remote(dst.at[2 * d], dst.at[2 * d], ss.at[2 * d], rs.at[2 * d], (z, mate, y)).wait_recv()
         send(dst.at[2 * d], dst.at[2 * d + 1], ss.at[2 * d + 1], rs.at[2 * d + 1], (z, mate, y))
 
+    def wo_came(slot, part, way):
+        remote(wo_all.at[slot, part], wo_all.at[slot, part], wo_s.at[slot, way], wo_r.at[slot, way],
+               (z, mate, y)).wait_recv()
+
+    def wo_send(slot, part, way, to, dev):
+        send(wo_all.at[slot, part], wo_all.at[to, part], wo_s.at[to, way], wo_r.at[to, way], dev)
+
+    def turn(slot):
+        half_rows = wo_ref.shape[1]
+        for i in range(2):
+            wo_t[slot, :, i * half_rows:(i + 1) * half_rows] = (wo_ref[i] if slot == 0 else wo_all[slot, i]).T
+
     def arrived(dst, ss, rs, slot):
         remote(dst.at[slot], dst.at[slot], ss.at[slot], rs.at[slot], (z, mate, y)).wait_recv()
 
@@ -109,7 +117,9 @@
         d, s = slot // 2, slot % 2
         return ((x - d + n_x) % n_x) * 2 + (c if s == 0 else 1 - c)
 
-    spread(tok_ref, tok_all, tok_s, tok_r)
+    for d in range(1, n_x):
+        send(tok_ref, tok_all.at[2 * d], tok_s.at[2 * d], tok_r.at[2 * d], (z, ((x + d) % n_x) * 2 + c, y))
+    send(tok_ref, tok_all.at[1], tok_s.at[1], tok_r.at[1], (z, mate, y))
     for d in range(1, n_req):
         send(own_all.at[0], own_all.at[d], ow_s.at[d], ow_r.at[d], ((z + d) % n_req, rho, y))
 
@@ -139,6 +149,7 @@
     project(0)
     arrived(tok_all, tok_s, tok_r, 1)
     project(1)
+    send(wo_ref, wo_all.at[1], wo_s.at[1, 0], wo_r.at[1, 0], (z, mate, y))
 
     step = min(1024, t_len)
 
@@ -186,16 +197,25 @@
         state(h)
         if h > 0:
             choose(h - 1)
-        if h == half:
+        if h == half - 1:
             for d in range(1, n_x):
                 forward(tok_all, tok_s, tok_r, d)
+                send(wo_ref.at[b], wo_all.at[2 * d, b], wo_s.at[2 * d, 0], wo_r.at[2 * d, 0],
+                     (z, ((x + d) % n_x) * 2 + c, y))
                 project(2 * d)
-            spread(wo_t, wo_all, wo_s, wo_r)
-        if h == heads - 1:
+        if h == half:
             for d in range(1, n_x):
                 arrived(tok_all, tok_s, tok_r, 2 * d + 1)
                 project(2 * d + 1)
     choose(heads - 1)
+    turn(0)
+    remote(wo_ref, wo_all.at[1], wo_s.at[1, 0], wo_r.at[1, 0], (z, mate, y)).wait_recv()
+    turn(1)
+    for d in range(1, n_x):
+        wo_came(2 * d, b, 0)
+        wo_send(2 * d, b, 1, 2 * d, (z_mate, rho, y))
+        wo_send(2 * d, b, 0, 2 * d + 1, (z, mate, y))
+
     for j in range(halves):
         total = own_part[j].astype(F32)
         for d in range(1, n_col):
@@ -244,9 +264,6 @@
             weights = jnp.where(si <= ti, weights, 0.0).astype(BF)
             inner[h, :, t:keep] = jnp.dot(v[:, :keep], weights, preferred_element_type=F32)
 
-    for d in range(1, n_x):
-        forward(wo_all, wo_s, wo_r, d)
-
     for h in range(heads):
         feats = products(proj[h * width:h * width + FEAT].astype(F32), 0.25, 1.0 / 32, 1.0 / 16, 0.125)
         for d in range(1, n_req):
@@ -265,16 +282,22 @@
         scatter(0, h)
         if h > 0:
             pass_on(h - 1)
+    for d in range(1, n_x):
+        wo_came(2 * d, 1 - b, 1)
+        wo_send(2 * d, 1 - b, 1, 2 * d + 1, (z, mate, y))
+        turn(2 * d)
     pass_on(heads - 1)
-    total = jnp.dot(wo_t[...], hid[rho], preferred_element_type=F32)
+    for d in range(1, n_x):
+        wo_came(2 * d + 1, b, 0)
+        wo_came(2 * d + 1, 1 - b, 1)
+        turn(2 * d + 1)
+    total = jnp.dot(wo_t[0], hid[rho], preferred_element_type=F32)
     for slot in range(1, n_row):
         src = slot_row(slot)
-        if slot % 2:
-            arrived(wo_all, wo_s, wo_r, slot)
         for h in range(heads):
             cols = pl.ds(h * HD, HD)
             remote(nrm.at[0, h, 0], hid.at[src, cols], hid_s.at[0, h, 0], hid_r.at[src, h], (z, rho, y)).wait_recv()
-        total += jnp.dot(wo_all[slot], hid[src], preferred_element_type=F32)
+        total += jnp.dot(wo_t[slot], hid[src], preferred_element_type=F32)
     out_ref[...] = total
 
     for copy in sent:
@@ -306,14 +329,14 @@
     vm = pltpu.VMEM
     dma = pltpu.SemaphoreType.DMA
     scratch = [
-        vm((dk, tr), BF), vm((rows, wide), BF), vm((rows, 8), F32), vm((heads, HD, SLOTS), F32),
-        vm((n_row, dk, tr), BF), vm((n_row, wide, rows), BF), vm((qkv, dk), BF), vm((wide, rows), BF),
+        vm((dk, tr), BF), vm((2, rows // 2, wide), BF), vm((rows, 8), F32), vm((heads, HD, SLOTS), F32),
+        vm((n_row, dk, tr), BF), vm((n_row, 2, rows // 2, wide), BF), vm((qkv, dk), BF), vm((n_row, wide, rows), BF),
         vm((heads, n_pref, FEAT, t_len), BF), vm((heads, n_pref, HD, t_len), BF),
         vm((halves, qkv, tr), BF), vm((n_row, qkv, tr), BF), vm((n_col, halves, qkv, tr), BF), vm((qkv, SLOTS), BF),
         vm((heads, n_pref, NF, HD), BF), vm((n_col, heads, n_pref, NF, HD), BF),
         vm((n_req, heads, NF, HD), BF), vm((n_req, heads, NF, HD), BF), vm((n_req, 8, 128), jnp.int32),
         vm((n_col, heads, halves, HD, tr), BF), vm((n_row, rows, tr), BF),
-        dma((3,)), dma((heads,)), dma((heads,)), dma((n_row,)), dma((n_row,)), dma((n_row,)), dma((n_row,)),
+        dma((3,)), dma((heads,)), dma((heads,)), dma((n_row,)), dma((n_row,)), dma((n_row, 2)), dma((n_row, 2)),
         dma((n_row,)), dma((n_col, halves)), dma((n_col, heads)), dma((n_col, heads)),
         dma((n_req, heads)), dma((n_req, heads)), dma((n_req,)), dma((n_req,)),
         dma((n_col, heads)), dma((n_col, heads)), dma((n_col, heads, halves)), dma((n_row, heads)),
@@ -329,7 +352,7 @@
         scratch_shapes=scratch,
         compiler_params=pltpu.CompilerParams(collective_id=0, has_side_effects=True,
                                              vmem_limit_bytes=60 * 1024 * 1024),
-    )(tokens, qkv_weight.T, out_weight, head_gain[None, :], prefix_keys, prefix_values, suffix_len, prefix_owner)
+    )(tokens, qkv_weight.T, out_weight.reshape(2, rows // 2, wide), head_gain[None, :], prefix_keys, prefix_values, suffix_len, prefix_owner)
     return (tokens.astype(F32) + mixed).astype(BF)
 
 

time: 68.2 us -> 66 us (0.968)
  Pallas kernels: 64.2 us -> 61.8 us
    pallas_call x1, Pallas kernels: 64.2 us -> 61.8 us  [shards(): pl.pallas_call(functools.partial(body, dims), out_shape=jax.ShapeDtypeStr...]
where the time goes in v4:
time: 66 us; the launch traced here: 65.2 us
  Pallas kernels  61.8 us (94%)
  other arithmetic  2.04 us (3%)
  between operations  1.37 us (2%)
    pallas_call x1, Pallas kernels, shards(): pl.pallas_call(functools.partial(body, dims), out_shape=jax.ShapeDtypeStr...  61.8 us
    convert_element_type x1, other arithmetic, shards(): return (tokens.astype(F32) + mixed).astype(BF)  2.04 us

profile of v4, /device:TPU:0, one launch (start us, length us, event | category | flops | bytes accessed | tf_op | source)
XLA Modules:
  0.0 65.2 jit_solution(15697740842204142507)
XLA Ops:
  0.0 0.0 copy-start
  1.4 61.8 %shard_map.82 = f32[896,256]{1,0:T(8,128)} custom-call(bf16[896,256]{1,0:T(8,128)(2,1)} %tok_any.1, bf16[576,896]{1,0:T(8,128)(2,1)} %bitcast.3, bf16[2,224,896]{2,1,0:T(8,128)(2,1)} %bitcast.4, f32[1,448]{1,0:T(1,128)} %bitcast.5, bf16[3,64,4096]{2,1,0:T(8,128)(2,1)} %keys_ref.1, bf16[3,448,4096]{2,1,0:T(8,128)(2,1)} %vals_ref.1, s32[1]{0:T(128)S(6)} %copy.9.len_ref, ...), custom_call_target="tpu_custom_call" | custom-call | tf_op jit(solution)/shard_map/pallas_call | solution.py:347
  63.2 0.0 copy-done
  63.2 2.0 %add_convert_fusion = bf16[896,256]{1,0:T(8,128)(2,1)} fusion(f32[896,256]{1,0:T(8,128)} %shard_map.82, bf16[896,256]{1,0:T(8,128)(2,1)S(1)} %copy-done), kind=kLoop, calls=%fused_computation | loop fusion | flops 688128 | bytes 1835008 | tf_op jit(solution)/shard_map/convert_element_type | solution.py:356
Async XLA Ops:
  0.0 63.2 %copy-start = (bf16[896,256]{1,0:T(8,128)(2,1)S(1)}, bf16[896,256]{1,0:T(8,128)(2,1)}, u32[]{:S(2)}) copy-start(bf16[896,256]{1,0:T(8,128)(2,1)} %tok_any.1) | copy-start | bytes 1376260

commit v5 on v4

--- a/solution.py
+++ b/solution.py
@@ -21,18 +21,9 @@
     parts = [(u * linear).astype(BF), (u * u * diag).astype(BF)]
     left = u * cross
     for s in range(1, 8):
-        parts.append((left * pltpu.roll(u, s, 0)).astype(BF))
+        rolled = jnp.concatenate([u[s:], u[:s]], axis=0)
+        parts.append((left * rolled).astype(BF))
     last = jnp.concatenate([left[:8] * u[8:], jnp.full((8, u.shape[1]), const, F32)], axis=0)
-    parts.append(last.astype(BF))
-    return jnp.concatenate(parts, axis=0)
-
-
-def key_products(rows):
-    u = rows.astype(F32)
-    parts = [rows, rows * rows]
-    for s in range(1, 8):
-        parts.append(rows * pltpu.roll(u, s, 0).astype(BF))
-    last = jnp.concatenate([u[:8] * u[8:], jnp.full((8, u.shape[1]), 1.0, F32)], axis=0)
     parts.append(last.astype(BF))
     return jnp.concatenate(parts, axis=0)
 
@@ -160,7 +151,7 @@
         def one(p, carry):
             total = jnp.zeros((NF, HD), F32)
             for t in range(0, t_len, step):
-                feats = key_products(keys_v[h, p, :, t:t + step])
+                feats = products(keys_v[h, p, :, t:t + step].astype(F32), 1.0, 1.0, 1.0, 1.0)
                 total += lax.dot_general(feats, vals_v[h, p, :, t:t + step], (((1,), (1,)), ((), ())),
                                          preferred_element_type=F32)
             st_part[h, p] = total.astype(BF)

time: 66 us -> 66 us (level)
  no operation moved by 1% of the time
where the time goes in v5:
time: 66 us; the launch traced here: 65.2 us
  Pallas kernels  61.8 us (94%)
  other arithmetic  2.04 us (3%)
  between operations  1.37 us (2%)
    pallas_call x1, Pallas kernels, shards(): pl.pallas_call(functools.partial(body, dims), out_shape=jax.ShapeDtypeStr...  61.8 us
    convert_element_type x1, other arithmetic, shards(): return (tokens.astype(F32) + mixed).astype(BF)  2.04 us

profile of v5, /device:TPU:0, one launch (start us, length us, event | category | flops | bytes accessed | tf_op | source)
XLA Modules:
  0.0 65.2 jit_solution(3517339068784007063)
XLA Ops:
  0.0 0.0 copy-start
  1.4 61.8 %shard_map.82 = f32[896,256]{1,0:T(8,128)} custom-call(bf16[896,256]{1,0:T(8,128)(2,1)} %tok_any.1, bf16[576,896]{1,0:T(8,128)(2,1)} %bitcast.3, bf16[2,224,896]{2,1,0:T(8,128)(2,1)} %bitcast.4, f32[1,448]{1,0:T(1,128)} %bitcast.5, bf16[3,64,4096]{2,1,0:T(8,128)(2,1)} %keys_ref.1, bf16[3,448,4096]{2,1,0:T(8,128)(2,1)} %vals_ref.1, s32[1]{0:T(128)S(6)} %copy.9.len_ref, ...), custom_call_target="tpu_custom_call" | custom-call | tf_op jit(solution)/shard_map/pallas_call | solution.py:338
  63.2 0.0 copy-done
  63.2 2.0 %add_convert_fusion = bf16[896,256]{1,0:T(8,128)(2,1)} fusion(f32[896,256]{1,0:T(8,128)} %shard_map.82, bf16[896,256]{1,0:T(8,128)(2,1)S(1)} %copy-done), kind=kLoop, calls=%fused_computation | loop fusion | flops 688128 | bytes 1835008 | tf_op jit(solution)/shard_map/convert_element_type | solution.py:347
Async XLA Ops:
  0.0 63.2 %copy-start = (bf16[896,256]{1,0:T(8,128)(2,1)S(1)}, bf16[896,256]{1,0:T(8,128)(2,1)}, u32[]{:S(2)}) copy-start(bf16[896,256]{1,0:T(8,128)(2,1)} %tok_any.1) | copy-start | bytes 1376260
